TPU v7x, 32 devices: a whole 2x2x4 slice. The times are simulated.
32 devices in a mesh: dp: 4 (over y, x), expert: 8 (over z, core).
Axes of the slice: x: 2, y: 2, z: 4, core: 2. Of those that a mesh axis runs over, the one named last changes fastest.
Arguments:
- activations: bfloat16 [4096, 4096], P(('dp', 'expert')), may hold values from -6 to 6
- cotangent: bfloat16 [4096, 4096], P(('dp', 'expert')), may hold values from -6 to 6
- basis: bfloat16 [4096, 512], replicated, may hold values from -0.09375 to 0.09375
- route_ids: int32 [4096, 8], P(('dp', 'expert')), may hold values from 0 to 15, all different within a row; in each aligned block of 128 rows (0 to 127, 128 to 255, ...) at most 96 rows name the same one
- route_weights: float32 [4096, 8], P(('dp', 'expert')), may hold values from 0.05 to 0.5
- proj_in: bfloat16 [16, 512, 128], P('expert'), may hold values from -0.25 to 0.25
- gate_factor: bfloat16 [16, 128, 1536], P('expert'), may hold values from -0.5 to 0.5
- up_factor: bfloat16 [16, 128, 1536], P('expert'), may hold values from -0.5 to 0.5
- down_factor: bfloat16 [16, 1536, 128], P('expert'), may hold values from -0.15625 to 0.15625
- proj_out: bfloat16 [16, 128, 512], P('expert'), may hold values from -0.5 to 0.5
Outputs:
- grad_input: bfloat16 [4096, 4096], P(('dp', 'expert'))
- grad_route: float32 [4096, 8], P(('dp', 'expert'))
- grad_basis: float32 [4096, 512], P(('dp', 'expert'))
- grad_proj_in: float32 [16, 512, 128], P('expert', 'dp')
- grad_gate: float32 [16, 128, 1536], P('expert', None, 'dp')
- grad_up: float32 [16, 128, 1536], P('expert', None, 'dp')
- grad_down: float32 [16, 1536, 128], P('expert', 'dp')
- grad_proj_out: float32 [16, 128, 512], P('expert', None, 'dp')
Inputs may be any that keep to these rules, and one draw needn't show every extreme that they name: `route_ids`: among the 128 rows of one device no expert is named by more than 96 of them, a bound that some block reaches; each row names 8 different experts.
All inputs are finite; a program needn't handle non-finite values.
Results may differ from a plain program's by a relative error of at most 0.025.
Values may be sent and summed in bfloat16 or wider, within the bound.
A program may use at most 128 MiB of HBM per device.

v0:
```python
import jax
import jax.numpy as jnp
from jax import lax
from jax.sharding import PartitionSpec as P

TOP = 8
EXP_DEV = 2
TOK_DEV = 128


def silu_parts(pre):
    sig = jax.nn.sigmoid(pre)
    return (pre * sig, sig * (1.0 + pre * (1.0 - sig)))


def per_device(
    activations,
    cotangent,
    basis,
    route_ids,
    route_weights,
    proj_in,
    gate_factor,
    up_factor,
    down_factor,
    proj_out,
):
    f32 = jnp.float32
    bf16 = jnp.bfloat16
    n_expert = lax.axis_size("expert")
    experts = EXP_DEV * n_expert
    capacity = max(2, 3 * TOK_DEV * TOP // (2 * experts))
    width = basis.shape[1]
    coords = jnp.dot(activations, basis, preferred_element_type=f32).astype(bf16)
    back = jnp.dot(cotangent, basis, preferred_element_type=f32).astype(bf16)
    flat_ids = route_ids.reshape(-1)
    onehot = (flat_ids[:, None] == jnp.arange(experts, dtype=jnp.int32)[None, :]).astype(jnp.int32)
    slots = jnp.sum(jnp.cumsum(onehot, axis=0) * onehot, axis=1) - 1
    place = flat_ids * capacity + slots
    weights = route_weights.reshape(-1)
    back_rep = jnp.repeat(back, TOP, axis=0)
    coord_rep = jnp.repeat(coords, TOP, axis=0)
    scaled_rep = (weights[:, None] * back_rep.astype(f32)).astype(bf16)
    send_coords = jnp.zeros((experts * capacity, width), bf16).at[place].set(coord_rep)
    send_scaled = jnp.zeros((experts * capacity, width), bf16).at[place].set(scaled_rep)
    send_coords = send_coords.reshape(n_expert, EXP_DEV * capacity, width)
    send_scaled = send_scaled.reshape(n_expert, EXP_DEV * capacity, width)
    got_coords, got_scaled = (
        lax.all_to_all(send_coords, "expert", split_axis=0, concat_axis=0, tiled=True),
        lax.all_to_all(send_scaled, "expert", split_axis=0, concat_axis=0, tiled=True),
    )
    rows = got_coords.reshape(n_expert, EXP_DEV, capacity, width)
    scaled = got_scaled.reshape(n_expert, EXP_DEV, capacity, width)
    codes = jnp.einsum("secr,erk->seck", rows, proj_in, preferred_element_type=f32).astype(bf16)
    gate_pre = jnp.einsum("seck,ekf->secf", codes, gate_factor, preferred_element_type=f32)
    up_pre = jnp.einsum("seck,ekf->secf", codes, up_factor, preferred_element_type=f32)
    active, slope = silu_parts(gate_pre)
    hidden = (active * up_pre).astype(bf16)
    narrow = jnp.einsum("secf,efk->seck", hidden, down_factor, preferred_element_type=f32).astype(
        bf16
    )
    outcome = jnp.einsum("seck,ekr->secr", narrow, proj_out, preferred_element_type=f32).astype(
        bf16
    )
    g_out = jnp.einsum("seck,secr->ekr", narrow, scaled, preferred_element_type=f32)
    d_narrow = jnp.einsum("secr,ekr->seck", scaled, proj_out, preferred_element_type=f32).astype(
        bf16
    )
    g_down = jnp.einsum("secf,seck->efk", hidden, d_narrow, preferred_element_type=f32)
    d_hidden = jnp.einsum("seck,efk->secf", d_narrow, down_factor, preferred_element_type=f32)
    d_gate = (d_hidden * up_pre * slope).astype(bf16)
    d_up = (d_hidden * active).astype(bf16)
    g_gate = jnp.einsum("seck,secf->ekf", codes, d_gate, preferred_element_type=f32)
    g_up = jnp.einsum("seck,secf->ekf", codes, d_up, preferred_element_type=f32)
    d_codes = (
        jnp.einsum("secf,ekf->seck", d_gate, gate_factor, preferred_element_type=f32)
        + jnp.einsum("secf,ekf->seck", d_up, up_factor, preferred_element_type=f32)
    ).astype(bf16)
    g_in = jnp.einsum("secr,seck->erk", rows, d_codes, preferred_element_type=f32)
    d_coords = jnp.einsum("seck,erk->secr", d_codes, proj_in, preferred_element_type=f32).astype(
        bf16
    )
    send_grad = d_coords.reshape(n_expert, EXP_DEV * capacity, width)
    send_out = outcome.reshape(n_expert, EXP_DEV * capacity, width)
    got_grad, got_out = (
        lax.all_to_all(send_grad, "expert", split_axis=0, concat_axis=0, tiled=True),
        lax.all_to_all(send_out, "expert", split_axis=0, concat_axis=0, tiled=True),
    )
    grad_rows = got_grad.reshape(experts * capacity, width)[place].astype(f32)
    out_rows = got_out.reshape(experts * capacity, width)[place].astype(f32)
    grad_route = jnp.sum(back_rep.astype(f32) * out_rows, axis=1).reshape(TOK_DEV, TOP)
    dz = jnp.sum(grad_rows.reshape(TOK_DEV, TOP, width), axis=1).astype(bf16)
    mixed = jnp.sum((weights[:, None] * out_rows).reshape(TOK_DEV, TOP, width), axis=1).astype(bf16)
    grad_input = lax.dot_general(
        dz, basis, (((1,), (1,)), ((), ())), preferred_element_type=f32
    ).astype(bf16)
    grad_basis = lax.psum_scatter(
        jnp.einsum("td,tr->dr", activations, dz, preferred_element_type=f32)
        + jnp.einsum("td,tr->dr", cotangent, mixed, preferred_element_type=f32),
        ("dp", "expert"),
        scatter_dimension=0,
        tiled=True,
    )
    grad_proj_in, grad_gate, grad_up, grad_down, grad_proj_out = (
        lax.psum_scatter(g_in.astype(jnp.bfloat16), "dp", scatter_dimension=1, tiled=True).astype(
            jnp.float32
        ),
        lax.psum_scatter(g_gate.astype(jnp.bfloat16), "dp", scatter_dimension=2, tiled=True).astype(
            jnp.float32
        ),
        lax.psum_scatter(g_up.astype(jnp.bfloat16), "dp", scatter_dimension=2, tiled=True).astype(
            jnp.float32
        ),
        lax.psum_scatter(g_down.astype(jnp.bfloat16), "dp", scatter_dimension=1, tiled=True).astype(
            jnp.float32
        ),
        lax.psum_scatter(g_out.astype(jnp.bfloat16), "dp", scatter_dimension=2, tiled=True).astype(
            jnp.float32
        ),
    )
    return (
        grad_input,
        grad_route,
        grad_basis,
        grad_proj_in,
        grad_gate,
        grad_up,
        grad_down,
        grad_proj_out,
    )


def solution(mesh):
    in_specs = (
        P(("dp", "expert"), None),
        P(("dp", "expert"), None),
        P(),
        P(("dp", "expert"), None),
        P(("dp", "expert"), None),
        P("expert", None, None),
        P("expert", None, None),
        P("expert", None, None),
        P("expert", None, None),
        P("expert", None, None),
    )
    out_specs = (
        P(("dp", "expert"), None),
        P(("dp", "expert"), None),
        P(("dp", "expert"), None),
        P("expert", "dp", None),
        P("expert", None, "dp"),
        P("expert", None, "dp"),
        P("expert", "dp", None),
        P("expert", None, "dp"),
    )
    return jax.shard_map(
        per_device, mesh=mesh, in_specs=in_specs, out_specs=out_specs, check_vma=False
    )
```

profile of v0, /device:TPU:0, one launch (start us, length us, event | category | flops | bytes accessed | tf_op | source)
XLA Modules:
  0.0 454.8 jit_solution(987830608108051508)
XLA Ops:
  9.1 4.5 reduce-window.6
  17.2 6.4 %scatter_custom_fusion.1 = bf16[1536,512]{1,0:T(8,128)(2,1)} fusion(s32[1024]{0:T(1024)S(1)} %bitcast.216, bf16[]{:T(256)} %constant.7.clone.1, bf16[128,512]{1,0:T(8,128)(2,1)S(1)} %convolution_convert_fusion.4), kind=kCustom, calls=%fused_computation.62 | custom fusion | bytes 1703938 | tf_op jit(solution)/shard_map/scatter | solution.py:44
  23.6 6.3 %all-to-all-start.1 = ((bf16[8,192,512]{2,1,0:T(8,128)(2,1)}), bf16[8,192,512]{2,1,0:T(8,128)(2,1)}, u32[]{:S(2)}, u32[]{:S(2)}) async-start(bf16[8,192,512]{2,1,0:T(8,128)(2,1)} %bitcast.14), calls=%async_computation.1 | async-start | bytes 3145728 | tf_op jit(solution)/shard_map/all_to_all | solution.py:49
  33.1 6.8 %scatter_custom_fusion = bf16[1536,512]{1,0:T(8,128)(2,1)} fusion(s32[1024]{0:T(1024)S(1)} %bitcast.217, f32[128,512]{1,0:T(8,128)S(1)} %fusion.46, f32[1024]{0:T(1024)S(1)} %mul.70, bf16[]{:T(256)} %constant.7.clone.1), kind=kCustom, calls=%fused_computation.60 | custom fusion | flops 1048576 | bytes 1839106 | tf_op jit(solution)/shard_map/scatter | solution.py:45
  39.9 27.9 %all-to-all-done.1 = bf16[8,192,512]{2,1,0:T(8,128)(2,1)} async-done(((bf16[8,192,512]{2,1,0:T(8,128)(2,1)}), bf16[8,192,512]{2,1,0:T(8,128)(2,1)}, u32[]{:S(2)}, u32[]{:S(2)}) %all-to-all-start.1) | async-done | bytes 1572896 | tf_op jit(solution)/shard_map/all_to_all | solution.py:49
  67.8 4.6 %all-to-all-start = ((bf16[8,192,512]{2,1,0:T(8,128)(2,1)}), bf16[8,192,512]{2,1,0:T(8,128)(2,1)}, u32[]{:S(2)}, u32[]{:S(2)}) async-start(bf16[8,192,512]{2,1,0:T(8,128)(2,1)} %bitcast.5), calls=%async_computation | async-start | bytes 3145728 | tf_op jit(solution)/shard_map/all_to_all | solution.py:50
  74.4 35.7 %all-to-all-done = bf16[8,192,512]{2,1,0:T(8,128)(2,1)} async-done(((bf16[8,192,512]{2,1,0:T(8,128)(2,1)}), bf16[8,192,512]{2,1,0:T(8,128)(2,1)}, u32[]{:S(2)}, u32[]{:S(2)}) %all-to-all-start) | async-done | bytes 1572896 | tf_op jit(solution)/shard_map/all_to_all | solution.py:50
  112.1 5.0 %fusion.58 = f32[2,8,96,1536]{3,2,1,0:T(8,128)} fusion(bf16[8,2,96,128]{3,2,0,1:T(8,128)(2,1)S(1)} %fusion.43, bf16[2,1536,128]{2,1,0:T(8,128)(2,1)S(1)} %copy-done.7), kind=kOutput, calls=%fused_computation.73 | convolution fusion | flops 603979776 | bytes 10616832 | tf_op jit(solution)/shard_map/seck,efk->secf/dot_general | solution.py:70
  117.2 5.0 %fusion.55 = f32[2,8,96,1536]{3,2,1,0:T(8,128)} fusion(bf16[8,2,96,128]{3,2,0,1:T(8,128)(2,1)S(1)} %fusion.40, bf16[2,128,1536]{2,1,0:T(8,128)(2,1)S(1)} %copy-done.6), kind=kOutput, calls=%fused_computation.70 | convolution fusion | flops 603979776 | bytes 10616832 | tf_op jit(solution)/shard_map/seck,ekf->secf/dot_general | solution.py:55
  122.2 10.4 %fusion.7 = (bf16[8,2,96,1536]{3,2,0,1:T(8,128)(2,1)}, bf16[8,2,96,1536]{3,2,0,1:T(8,128)(2,1)S(1)}, bf16[8,2,96,1536]{3,2,0,1:T(8,128)(2,1)S(1)}) fusion(f32[2,8,96,1536]{3,2,1,0:T(8,128)} %fusion.55, f32[2,8,96,1536]{3,2,1,0:T(8,128)} %fusion.58, bf16[8,2,96,128]{3,2,0,1:T(8,128)(2,1)S(1)} %fusion.40, bf16[2,128,1536]{2,1,0:T(8,128)(2,1)S(1)} %copy-done.12), kind=kOutput, calls=%fused_computation.16 | convolution fusion | flops 639369216 | bytes 34209792 | tf_op jit(solution)/shard_map/seck,ekf->secf/dot_general | solution.py:56
  141.7 3.9 fusion.39
  154.7 4.1 fusion.9
  166.8 12.6 %all-to-all-done.2 = bf16[8,192,512]{2,1,0:T(8,128)(2,1)S(1)} async-done(((bf16[8,192,512]{2,1,0:T(8,128)(2,1)}), bf16[8,192,512]{2,1,0:T(8,128)(2,1)S(1)}, u32[]{:S(2)}, u32[]{:S(2)}) %all-to-all-start.2) | async-done | bytes 1572896 | tf_op jit(solution)/shard_map/all_to_all | solution.py:86
  179.4 4.3 all-to-all-start.3
  183.8 4.1 fusion.10
  191.2 5.3 %fusion.11 = bf16[2,1536,128]{2,1,0:T(8,128)(2,1)} fusion(bf16[8,2,96,1536]{3,2,0,1:T(8,128)(2,1)} %get-tuple-element.32, bf16[8,2,96,128]{3,2,0,1:T(8,128)(2,1)} %copy-done.11), kind=kOutput, calls=%fused_computation.29 | convolution fusion | flops 604372992 | bytes 5898240 | tf_op jit(solution)/shard_map/secf,seck->efk/dot_general | solution.py:69
  196.5 5.1 %gather_fusion = bf16[1024,512]{1,0:T(8,128)(2,1)} fusion(bf16[1536,512]{1,0:T(8,128)(2,1)S(1)} %bitcast.202, s32[1024]{0:T(1024)S(1)} %broadcast_clamp_fusion), kind=kCustom, calls=%fused_computation | custom fusion | bytes 2101248 | tf_op jit(solution)/shard_map/gather | solution.py:89
  201.6 19.9 %all-to-all-done.3 = bf16[8,192,512]{2,1,0:T(8,128)(2,1)} async-done(((bf16[8,192,512]{2,1,0:T(8,128)(2,1)}), bf16[8,192,512]{2,1,0:T(8,128)(2,1)}, u32[]{:S(2)}, u32[]{:S(2)}) %all-to-all-start.3) | async-done | bytes 1572896 | tf_op jit(solution)/shard_map/all_to_all | solution.py:87
  221.6 5.7 %gather_fusion.1 = bf16[1024,512]{1,0:T(8,128)(2,1)S(1)} fusion(bf16[1536,512]{1,0:T(8,128)(2,1)} %bitcast.36, s32[1024]{0:T(1024)S(1)} %broadcast_clamp_fusion), kind=kCustom, calls=%fused_computation.1 | custom fusion | bytes 2101248 | tf_op jit(solution)/shard_map/gather | solution.py:90
  230.0 4.5 add_bitcast_fusion
  238.9 24.1 %reduce-scatter.21.cloned.1.call-done = bf16[384,256]{1,0:T(8,128)(2,1)} async-done(((bf16[1536,256]{1,0:T(8,128)(2,1)}), bf16[384,256]{1,0:T(8,128)(2,1)}) %reduce-scatter.21.cloned.1.call-update) | async-done | bytes 196624
  265.7 26.2 %reduce-scatter.17.cloned.1.call-done = bf16[2,384,128]{2,1,0:T(8,128)(2,1)} async-done(((bf16[2,1536,128]{2,1,0:T(8,128)(2,1)}), bf16[2,384,128]{2,1,0:T(8,128)(2,1)}) %reduce-scatter.17.cloned.1.call-update) | async-done | bytes 196624 | tf_op jit(solution)/shard_map/reduce_scatter | solution.py:114
  294.6 4.6 %convolution_convert_fusion = bf16[128,4096]{1,0:T(8,128)(2,1)} fusion(bf16[128,512]{1,0:T(8,128)(2,1)S(1)} %bitcast_reduce_fusion, bf16[4096,512]{1,0:T(8,128)(2,1)} %param.12), kind=kOutput, calls=%fused_computation.20 | convolution fusion | flops 537395200 | bytes 5373952 | tf_op jit(solution)/shard_map/dot_general | solution.py:94
  299.2 146.9 %reduce-scatter.13.cloned.1.call-done = f32[128,512]{0,1:T(8,128)} async-done(((f32[4096,512]{0,1:T(8,128)}), f32[128,512]{0,1:T(8,128)}) %reduce-scatter.13.cloned.1.call-update) | async-done | bytes 262160 | tf_op jit(solution)/shard_map/reduce_scatter | solution.py:97
  (103 shorter events, 56.3 us)
Async XLA Ops:
  7.2 7.0 %copy-start = (bf16[128,4096]{1,0:T(8,128)(2,1)S(1)}, bf16[128,4096]{1,0:T(8,128)(2,1)}, u32[]{:S(2)}) copy-start(bf16[128,4096]{1,0:T(8,128)(2,1)} %param.10) | copy-start | bytes 3145732
  14.1 15.8 %copy-start.15 = (f32[128,8]{0,1:T(8,128)S(1)}, f32[128,8]{0,1:T(8,128)}, u32[]{:S(2)}) copy-start(f32[128,8]{0,1:T(8,128)} %param.14) | copy-start | bytes 12292
  14.2 15.9 %copy-start.4 = (bf16[128,4096]{1,0:T(8,128)(2,1)S(1)}, bf16[128,4096]{1,0:T(8,128)(2,1)}, u32[]{:S(2)}) copy-start(bf16[128,4096]{1,0:T(8,128)(2,1)} %param.11) | copy-start | bytes 3145732
  23.6 44.3 %all-to-all-start.1 = ((bf16[8,192,512]{2,1,0:T(8,128)(2,1)}), bf16[8,192,512]{2,1,0:T(8,128)(2,1)}, u32[]{:S(2)}, u32[]{:S(2)}) async-start(bf16[8,192,512]{2,1,0:T(8,128)(2,1)} %bitcast.14), calls=%async_computation.1 | async-start | bytes 3145728 | tf_op jit(solution)/shard_map/all_to_all | solution.py:49
  30.1 42.3 %copy-start.13 = (bf16[2,512,128]{2,1,0:T(8,128)(2,1)S(1)}, bf16[2,512,128]{2,1,0:T(8,128)(2,1)}, u32[]{:S(2)}) copy-start(bf16[2,512,128]{2,1,0:T(8,128)(2,1)} %param.15) | copy-start | bytes 786436
  33.1 79.0 %copy-start.8 = (f32[128,512]{1,0:T(8,128)}, f32[128,512]{1,0:T(8,128)S(1)}, u32[]{:S(2)}) copy-start(f32[128,512]{1,0:T(8,128)S(1)} %fusion.46) | copy-start | bytes 786436
  33.1 77.0 %copy-start.14 = (bf16[2,128,512]{2,1,0:T(8,128)(2,1)S(1)}, bf16[2,128,512]{2,1,0:T(8,128)(2,1)}, u32[]{:S(2)}) copy-start(bf16[2,128,512]{2,1,0:T(8,128)(2,1)} %param.19) | copy-start | bytes 786436
  67.8 44.3 %copy-start.7 = (bf16[2,1536,128]{2,1,0:T(8,128)(2,1)S(1)}, bf16[2,1536,128]{2,1,0:T(8,128)(2,1)}, u32[]{:S(2)}) copy-start(bf16[2,1536,128]{2,1,0:T(8,128)(2,1)} %param.18) | copy-start | bytes 2359300
  67.8 42.3 %all-to-all-start = ((bf16[8,192,512]{2,1,0:T(8,128)(2,1)}), bf16[8,192,512]{2,1,0:T(8,128)(2,1)}, u32[]{:S(2)}, u32[]{:S(2)}) async-start(bf16[8,192,512]{2,1,0:T(8,128)(2,1)} %bitcast.5), calls=%async_computation | async-start | bytes 3145728 | tf_op jit(solution)/shard_map/all_to_all | solution.py:50
  112.1 5.1 %copy-start.11 = (bf16[8,2,96,128]{3,2,0,1:T(8,128)(2,1)}, bf16[8,2,96,128]{3,2,0,1:T(8,128)(2,1)S(1)}, u32[]{:S(2)}) copy-start(bf16[8,2,96,128]{3,2,0,1:T(8,128)(2,1)S(1)} %fusion.43) | copy-start | bytes 1179652
  112.1 5.1 %copy-start.6 = (bf16[2,128,1536]{2,1,0:T(8,128)(2,1)S(1)}, bf16[2,128,1536]{2,1,0:T(8,128)(2,1)}, u32[]{:S(2)}) copy-start(bf16[2,128,1536]{2,1,0:T(8,128)(2,1)} %param.16) | copy-start | bytes 2359300
  117.2 5.0 %copy-start.12 = (bf16[2,128,1536]{2,1,0:T(8,128)(2,1)S(1)}, bf16[2,128,1536]{2,1,0:T(8,128)(2,1)}, u32[]{:S(2)}) copy-start(bf16[2,128,1536]{2,1,0:T(8,128)(2,1)} %param.17) | copy-start | bytes 2359300
  132.6 2.8 copy-start.1
  132.6 3.6 copy-start.2
  138.1 41.3 %all-to-all-start.2 = ((bf16[8,192,512]{2,1,0:T(8,128)(2,1)}), bf16[8,192,512]{2,1,0:T(8,128)(2,1)S(1)}, u32[]{:S(2)}, u32[]{:S(2)}) async-start(bf16[8,192,512]{2,1,0:T(8,128)(2,1)} %bitcast.203), calls=%async_computation.2 | async-start | bytes 3145728 | tf_op jit(solution)/shard_map/all_to_all | solution.py:86
  141.7 92.8 %reduce-scatter.23.cloned.1.call-start = ((), (), s32[]{:S(2)}) async-start(), calls=%async_computation.15 | async-start | bytes 327680
  151.7 84.5 %reduce-scatter.15.cloned.1.call-start = ((), (), s32[]{:S(2)}) async-start(), calls=%async_computation.11 | async-start | bytes 327680 | tf_op jit(solution)/shard_map/reduce_scatter | solution.py:105
  154.7 83.0 %reduce-scatter.19.cloned.1.call-start = ((), (), s32[]{:S(2)}) async-start(), calls=%async_computation.13 | async-start | bytes 983040
  179.4 42.1 %all-to-all-start.3 = ((bf16[8,192,512]{2,1,0:T(8,128)(2,1)}), bf16[8,192,512]{2,1,0:T(8,128)(2,1)}, u32[]{:S(2)}, u32[]{:S(2)}) async-start(bf16[8,192,512]{2,1,0:T(8,128)(2,1)} %bitcast.204), calls=%async_computation.3 | async-start | bytes 3145728 | tf_op jit(solution)/shard_map/all_to_all | solution.py:87
  183.7 79.2 %reduce-scatter.21.cloned.1.call-start = ((), (), s32[]{:S(2)}) async-start(), calls=%async_computation.14 | async-start | bytes 983040
  191.1 100.7 %reduce-scatter.17.cloned.1.call-start = ((), (), s32[]{:S(2)}) async-start(), calls=%async_computation.12 | async-start | bytes 983040 | tf_op jit(solution)/shard_map/reduce_scatter | solution.py:114
  196.5 249.7 %reduce-scatter.13.cloned.1.call-start = ((), (), s32[]{:S(2)}) async-start(), calls=%async_computation.10 | async-start | bytes 8650752 | tf_op jit(solution)/shard_map/reduce_scatter | solution.py:97
  221.6 5.7 %copy-start.3 = (bf16[1024,512]{1,0:T(8,128)(2,1)S(1)}, bf16[1024,512]{1,0:T(8,128)(2,1)}, u32[]{:S(2)}) copy-start(bf16[1024,512]{1,0:T(8,128)(2,1)} %gather_fusion) | copy-start | bytes 3145732
  234.5 59.1 %copy-start.9 = (f32[128,512]{1,0:T(8,128)S(1)}, f32[128,512]{1,0:T(8,128)}, u32[]{:S(2)}) copy-start(f32[128,512]{1,0:T(8,128)} %copy-done.8) | copy-start | bytes 786436
  (2 other events, 3.1 us)
Sparse Core Ops, SparseCore 0:
  151.8 25.4 reduce-scatter.22
  180.9 24.1 reduce-scatter.14
  207.9 26.0 reduce-scatter.18
  236.8 26.1 reduce-scatter.20
  265.7 26.0 reduce-scatter.16
  294.0 152.1 reduce-scatter.12
where the time goes:
time: 456 us; the launch traced here: 455 us
  waiting for transfers between devices  293 us (64%)
  matrix products  68.4 us (15%)
  local copies, waits for them, and re-layouts  40.1 us (9%)
  other arithmetic  19.3 us (4%)
  starting transfers between devices  19.1 us (4%)
  between operations  14.5 us (3%)
    reduce_scatter x1, waiting for transfers between devices, per_device(): lax.psum_scatter(jnp.einsum('td,tr->dr', activations, dz, preferred_eleme...  147 us
    all_to_all x1, waiting for transfers between devices, per_device(): lax.all_to_all(send_scaled, 'expert', split_axis=0, concat_axis=0, tiled=...  35.7 us
    all_to_all x1, waiting for transfers between devices, per_device(): lax.all_to_all(send_coords, 'expert', split_axis=0, concat_axis=0, tiled=...  27.9 us
    reduce_scatter x1, waiting for transfers between devices, per_device(): lax.psum_scatter(g_down.astype(jnp.bfloat16), 'dp', scatter_dimension=1,...  26.2 us
    unnamed x9, waiting for transfers between devices  24.2 us
    all_to_all x1, waiting for transfers between devices, per_device(): lax.all_to_all(send_out, 'expert', split_axis=0, concat_axis=0, tiled=True)  19.9 us
    unnamed x48, local copies, waits for them, and re-layouts  19.5 us
    all_to_all x1, waiting for transfers between devices, per_device(): lax.all_to_all(send_grad, 'expert', split_axis=0, concat_axis=0, tiled=True)  12.6 us
  transfers between devices with their start and end apart: 10, of which 7 were waited for; matrix products, arithmetic and copies ran while one was open for 18% of the time, Pallas kernels for 0%

commit v1 on v0

v1 whole, which is shorter than its diff:
```python
import functools

import jax
import jax.numpy as jnp
from jax import lax
from jax.experimental import pallas as pl
from jax.experimental.pallas import tpu as pltpu
from jax.sharding import PartitionSpec as P

EXP_DEV = 2
TOK_DEV = 128
LANES = 128
VMEM_LIMIT = 58 * 1024 * 1024
MESH = pl.DeviceIdType.MESH
f32 = jnp.float32
bf16 = jnp.bfloat16


def remote(src, dst, send, recv, **device):
    return pltpu.make_async_remote_copy(
        src_ref=src, dst_ref=dst, send_sem=send, recv_sem=recv, device_id=device, device_id_type=MESH
    )


def dot(a, b):
    return jnp.dot(a, b, preferred_element_type=f32)


def dot_nt(a, b):
    return lax.dot_general(a, b, (((1,), (1,)), ((), ())), preferred_element_type=f32)


def dot_tn(a, b):
    return lax.dot_general(a, b, (((0,), (0,)), ((), ())), preferred_element_type=f32)


def loop(low, high, body):
    def step(i, carry):
        body(i)
        return carry

    lax.fori_loop(low, high, step, 0)


def greet(n, n_dp, me, p):
    barrier = pltpu.get_barrier_semaphore()

    def expert_peer(d):
        pl.semaphore_signal(
            barrier, inc=1, device_id={"expert": lax.rem(me + d, n)}, device_id_type=MESH
        )

    def dp_peer(d):
        pl.semaphore_signal(
            barrier, inc=1, device_id={"dp": lax.rem(p + d, n_dp)}, device_id_type=MESH
        )

    loop(1, n, expert_peer)
    loop(1, n_dp, dp_peer)
    pl.semaphore_wait(barrier, n - 1 + n_dp - 1)


def gather_kernel(
    n, n_dp, act, cot, basis, wt, x_out, w_out, cols_out, s_c, r_c, s_x, r_x, s_f, s_w, r_w
):
    me, p = lax.axis_index("expert"), lax.axis_index("dp")
    nz = n // 2
    core, z = lax.rem(me, 2), me // 2
    sib = me + 1 - 2 * core
    width = act.shape[1] // n_dp
    greet(n, n_dp, me, p)

    def w_copy(d):
        return remote(
            wt.at[lax.rem(me + d, n)], w_out.at[me], s_w.at[d], r_w.at[me], expert=lax.rem(me + d, n)
        )

    loop(1, n, lambda d: w_copy(d).start())

    def x_copy(a, d, to):
        return remote(x_out.at[me, a], x_out.at[me, a], s_x.at[a, d], r_x.at[a, me], expert=to)

    def line_peer(d):
        return lax.rem(z + d, nz) * 2 + core

    for a, ref in enumerate((act, cot)):
        x_out[me, a] = dot(ref[...], basis[...]).astype(bf16)
        loop(1, nz, lambda d: x_copy(a, d, line_peer(d)).start())
        x_copy(a, 0, sib).start()

    def col_copy(a, d):
        q = lax.rem(p + d, n_dp)
        ref = (act, cot)[a]
        return remote(
            ref.at[:, pl.ds(pl.multiple_of(q * width, LANES), width)],
            cols_out.at[p, a],
            s_c.at[a, d],
            r_c.at[a, p],
            dp=q,
        )

    for a in range(2):
        loop(1, n_dp, lambda d: col_copy(a, d).start())
    for a, ref in enumerate((act, cot)):
        cols_out[p, a] = ref[:, pl.ds(pl.multiple_of(p * width, LANES), width)]
    w_out[me] = wt[me]

    def forward(a, d):
        src = lax.rem(z + nz - d, nz) * 2 + core
        return remote(x_out.at[src, a], x_out.at[src, a], s_f.at[a, d], r_x.at[a, src], expert=sib)

    def pass_on(a, d):
        forward(a, d).wait_recv()
        forward(a, d).start()

    for a in range(2):
        loop(1, nz, lambda d: pass_on(a, d))

    def sib_wait(a, k):
        src = k * 2 + 1 - core
        remote(
            x_out.at[src, a], x_out.at[src, a], s_f.at[a, 0], r_x.at[a, src], expert=sib
        ).wait_recv()

    def w_wait(d):
        src = lax.rem(me + n - d, n)
        remote(wt.at[src], w_out.at[src], s_w.at[d], r_w.at[src], expert=src).wait_recv()

    def col_wait(a, d):
        src = lax.rem(p + n_dp - d, n_dp)
        remote(cols_out.at[src, a], cols_out.at[src, a], s_c.at[a, d], r_c.at[a, src], dp=src).wait_recv()

    loop(1, n, w_wait)
    for a in range(2):
        loop(0, nz, lambda k: sib_wait(a, k))
        loop(1, n_dp, lambda d: col_wait(a, d))
    loop(1, n, lambda d: w_copy(d).wait_send())
    for a in range(2):
        x_copy(a, 0, sib).wait_send()
        loop(1, nz, lambda d: x_copy(a, d, line_peer(d)).wait_send())
        loop(1, nz, lambda d: forward(a, d).wait_send())
        loop(1, n_dp, lambda d: col_copy(a, d).wait_send())


def expert_kernel(n_dp, chunk, x, w, pin, gate, up, down, pout, part, route, packed, acc):
    step = pl.program_id(0)
    nb, rank = x.shape[0], x.shape[3]
    rows = nb * TOK_DEV
    ff = gate.shape[2]

    @pl.when(step == 0)
    def _():
        acc[...] = jnp.zeros_like(acc)

    coords = x[:, 0].reshape(rows, rank)
    back = x[:, 1].reshape(rows, rank).astype(f32)
    dz = jnp.zeros((rows, rank), f32)
    mixed = jnp.zeros((rows, rank), f32)
    dots = jnp.zeros((8, rows), f32)
    line = lax.broadcasted_iota(jnp.int32, (8, rows), 0)
    for e in range(EXP_DEV):
        we = w[:, e : e + 1]
        scaled = (we * back).astype(bf16)
        codes = dot(coords, pin[e]).astype(bf16)
        d_narrow32 = dot_nt(scaled, pout[e])
        d_narrow = d_narrow32.astype(bf16)
        codes_t, d_narrow_t = codes.T, d_narrow.T
        narrow32 = jnp.zeros((rows, LANES), f32)
        d_codes32 = jnp.zeros((rows, LANES), f32)
        for at in range(0, ff, chunk):
            now = slice(at, at + chunk)
            gate_pre = dot(codes, gate[e, :, now])
            up_pre = dot(codes, up[e, :, now])
            d_hidden = dot_nt(d_narrow, down[e, now, :])
            sig = 0.5 * jnp.tanh(0.5 * gate_pre) + 0.5
            active = gate_pre * sig
            slope = sig + active * (1.0 - sig)
            hidden = (active * up_pre).astype(bf16)
            d_gate = (d_hidden * up_pre * slope).astype(bf16)
            d_up = (d_hidden * active).astype(bf16)
            narrow32 += dot(hidden, down[e, now, :])
            d_codes32 += dot_nt(d_gate, gate[e, :, now]) + dot_nt(d_up, up[e, :, now])
            acc[e, :, at : at + chunk] += dot(codes_t, d_gate)
            acc[e, :, ff + at : ff + at + chunk] += dot(codes_t, d_up)
            acc[e, :, 2 * ff + at : 2 * ff + at + chunk] += dot(d_narrow_t, hidden)
        narrow = narrow32.astype(bf16)
        d_codes = d_codes32.astype(bf16)
        outcome = dot(narrow, pout[e]).astype(bf16)
        mixed += we * outcome.astype(f32)
        dz += dot_nt(d_codes, pin[e])
        acc[e, :, 3 * ff : 3 * ff + rank] += dot(d_codes.T, coords)
        acc[e, :, 3 * ff + rank :] += dot(narrow.T, scaled)
        product = narrow.astype(f32) * d_narrow32
        sums = lax.dot_general(
            jnp.ones((8, LANES), f32),
            product,
            (((1,), (1,)), ((), ())),
            precision=lax.Precision.HIGHEST,
            preferred_element_type=f32,
        )
        dots = jnp.where(line == e, sums, dots)
    part[:, 0] = dz.astype(bf16).reshape(nb, TOK_DEV, rank)
    part[:, 1] = mixed.astype(bf16).reshape(nb, TOK_DEV, rank)
    for b in range(nb):
        route[b] = dots[:, b * TOK_DEV : (b + 1) * TOK_DEV]

    @pl.when(step == pl.num_programs(0) - 1)
    def _():
        wide, deep = ff // n_dp, rank // n_dp
        for q in range(n_dp):
            for e in range(EXP_DEV):
                starts = [3 * ff + q * deep + i for i in range(0, deep, LANES)]
                for base in (0, ff, 2 * ff):
                    starts += [base + q * wide + i for i in range(0, wide, LANES)]
                starts += [3 * ff + rank + q * deep + i for i in range(0, deep, LANES)]
                for i, at in enumerate(starts):
                    packed[q, e, i] = acc[e, :, at : at + LANES].astype(bf16)


def expert_sum(n, me, part, held, landed, total, s1, r1, s2, r2):
    nz = n // 2
    core, z = lax.rem(me, 2), me // 2
    sib = me + 1 - 2 * core

    def to_sib(k):
        return remote(part.at[k * 2 + 1 - core], held.at[k], s1.at[k], r1.at[k], expert=sib)

    def to_line(d):
        k = lax.rem(z + d, nz)
        return remote(held.at[k], landed.at[z], s2.at[d], r2.at[z], expert=k * 2 + core)

    loop(1, nz, lambda d: to_sib(lax.rem(z + d, nz)).start())
    to_sib(z).start()

    def add(d):
        k = lax.rem(z + d, nz)
        to_sib(k).wait_recv()
        held[k] = (part[k * 2 + core].astype(f32) + held[k].astype(f32)).astype(bf16)
        to_line(d).start()

    loop(1, nz, add)
    to_sib(z).wait_recv()
    total[...] = part[me].astype(f32) + held[z].astype(f32)

    def collect(d):
        k = lax.rem(z + nz - d, nz)
        remote(held.at[k], landed.at[k], s2.at[d], r2.at[k], expert=k * 2 + core).wait_recv()
        total[...] += landed[k].astype(f32)

    loop(1, nz, collect)
    loop(0, nz, lambda k: to_sib(k).wait_send())
    loop(1, nz, lambda d: to_line(d).wait_send())


def combine_kernel(
    n,
    n_dp,
    part,
    route,
    packed,
    cols,
    basis,
    grad_input,
    grad_basis,
    grads,
    route_out,
    held,
    landed,
    total,
    dzm,
    block,
    held_b,
    landed_b,
    grads_in,
    s_g,
    r_g,
    s_r,
    r_r,
    s1,
    r1,
    s2,
    r2,
    s_d,
    r_d,
    t1,
    q1,
    t2,
    q2,
):
    me, p = lax.axis_index("expert"), lax.axis_index("dp")
    rank = basis.shape[1]
    greet(n, n_dp, me, p)

    def route_copy(d):
        j = lax.rem(me + d, n)
        return remote(route.at[j], route_out.at[me], s_r.at[d], r_r.at[me], expert=j)

    def grad_copy(d):
        q = lax.rem(p + d, n_dp)
        return remote(packed.at[q], grads_in.at[p], s_g.at[d], r_g.at[p], dp=q)

    loop(1, n, lambda d: route_copy(d).start())
    loop(1, n_dp, lambda d: grad_copy(d).start())
    route_out[me] = route[me]
    expert_sum(n, me, part, held, landed, total, s1, r1, s2, r2)
    dzm[p] = total[...].astype(bf16)

    def dzm_copy(d):
        q = lax.rem(p + d, n_dp)
        return remote(dzm.at[p], dzm.at[p], s_d.at[d], r_d.at[p], dp=q)

    loop(1, n_dp, lambda d: dzm_copy(d).start())
    grad_input[...] = dot_nt(dzm[p, 0], basis[...]).astype(bf16)

    def dzm_wait(d):
        src = lax.rem(p + n_dp - d, n_dp)
        remote(dzm.at[src], dzm.at[src], s_d.at[d], r_d.at[src], dp=src).wait_recv()

    loop(1, n_dp, dzm_wait)
    tokens = n_dp * 2 * TOK_DEV
    width = cols.shape[3]
    sums = dot_tn(cols[...].reshape(tokens, width), dzm[...].reshape(tokens, rank))
    block[...] = sums.astype(bf16).reshape(block.shape)
    expert_sum(n, me, block, held_b, landed_b, grad_basis, t1, q1, t2, q2)

    def grad_wait(d):
        src = lax.rem(p + n_dp - d, n_dp)
        remote(grads_in.at[src], grads_in.at[src], s_g.at[d], r_g.at[src], dp=src).wait_recv()
        grads[...] += grads_in[src].astype(f32)

    grads[...] = packed[p].astype(f32)
    loop(1, n_dp, grad_wait)

    def route_wait(d):
        src = lax.rem(me + n - d, n)
        remote(route.at[src], route_out.at[src], s_r.at[d], r_r.at[src], expert=src).wait_recv()

    loop(1, n, route_wait)
    loop(1, n, lambda d: route_copy(d).wait_send())
    loop(1, n_dp, lambda d: grad_copy(d).wait_send())
    loop(1, n_dp, lambda d: dzm_copy(d).wait_send())


def per_device(
    n,
    n_dp,
    activations,
    cotangent,
    basis,
    route_ids,
    route_weights,
    proj_in,
    gate_factor,
    up_factor,
    down_factor,
    proj_out,
):
    model, rank = basis.shape
    ff = gate_factor.shape[2]
    nz = n // 2
    experts = EXP_DEV * n
    width = model // n_dp
    vmem = pl.BlockSpec(memory_space=pltpu.VMEM)
    dma = pltpu.SemaphoreType.DMA

    chosen = route_ids[:, None, :] == jnp.arange(experts, dtype=jnp.int32)[None, :, None]
    dense = jnp.sum(jnp.where(chosen, route_weights[:, None, :], 0.0), axis=2)
    wt = dense.T.reshape(n, EXP_DEV, TOK_DEV)
    wt = jnp.pad(wt, ((0, 0), (0, 8 - EXP_DEV), (0, 0)))

    x, w_all, cols = pl.pallas_call(
        functools.partial(gather_kernel, n, n_dp),
        out_shape=(
            jax.ShapeDtypeStruct((n, 2, TOK_DEV, rank), bf16),
            jax.ShapeDtypeStruct((n, 8, TOK_DEV), f32),
            jax.ShapeDtypeStruct((n_dp, 2, TOK_DEV, width), bf16),
        ),
        in_specs=[vmem] * 4,
        out_specs=(vmem,) * 3,
        scratch_shapes=[
            dma((2, n_dp)),
            dma((2, n_dp)),
            dma((2, nz)),
            dma((2, n)),
            dma((2, nz)),
            dma((n,)),
            dma((n,)),
        ],
        compiler_params=pltpu.CompilerParams(
            collective_id=0, has_side_effects=True, vmem_limit_bytes=VMEM_LIMIT
        ),
        name="gather_tokens",
    )(activations, cotangent, basis, wt)

    w_rows = w_all.transpose(0, 2, 1).reshape(n * TOK_DEV, 8)
    nb = 2
    blocks = EXP_DEV, (2 * rank + 3 * ff) // n_dp // LANES, LANES, LANES
    whole = lambda a: pl.BlockSpec(a.shape, lambda i: (0,) * a.ndim)
    part, route, packed = pl.pallas_call(
        functools.partial(expert_kernel, n_dp, ff // 3),
        grid=(n // nb,),
        out_shape=(
            jax.ShapeDtypeStruct((n, 2, TOK_DEV, rank), bf16),
            jax.ShapeDtypeStruct((n, 8, TOK_DEV), f32),
            jax.ShapeDtypeStruct((n_dp, *blocks), bf16),
        ),
        in_specs=[
            pl.BlockSpec((nb, 2, TOK_DEV, rank), lambda i: (i, 0, 0, 0)),
            pl.BlockSpec((nb * TOK_DEV, 8), lambda i: (i, 0)),
            whole(proj_in),
            whole(gate_factor),
            whole(up_factor),
            whole(down_factor),
            whole(proj_out),
        ],
        out_specs=(
            pl.BlockSpec((nb, 2, TOK_DEV, rank), lambda i: (i, 0, 0, 0)),
            pl.BlockSpec((nb, 8, TOK_DEV), lambda i: (i, 0, 0)),
            pl.BlockSpec((n_dp, *blocks), lambda i: (0, 0, 0, 0, 0)),
        ),
        scratch_shapes=[pltpu.VMEM((EXP_DEV, LANES, 3 * ff + 2 * rank), f32)],
        compiler_params=pltpu.CompilerParams(vmem_limit_bytes=VMEM_LIMIT),
        name="experts",
    )(x, w_rows, proj_in, gate_factor, up_factor, down_factor, proj_out)

    rows_b = width // n
    grad_input, grad_basis, grads, route_got = pl.pallas_call(
        functools.partial(combine_kernel, n, n_dp),
        out_shape=(
            jax.ShapeDtypeStruct((TOK_DEV, model), bf16),
            jax.ShapeDtypeStruct((rows_b, rank), f32),
            jax.ShapeDtypeStruct(blocks, f32),
            jax.ShapeDtypeStruct((n, 8, TOK_DEV), f32),
        ),
        in_specs=[vmem] * 5,
        out_specs=(vmem,) * 4,
        scratch_shapes=[
            pltpu.VMEM((nz, 2, TOK_DEV, rank), bf16),
            pltpu.VMEM((nz, 2, TOK_DEV, rank), bf16),
            pltpu.VMEM((2, TOK_DEV, rank), f32),
            pltpu.VMEM((n_dp, 2, TOK_DEV, rank), bf16),
            pltpu.VMEM((n, rows_b, rank), bf16),
            pltpu.VMEM((nz, rows_b, rank), bf16),
            pltpu.VMEM((nz, rows_b, rank), bf16),
            pltpu.VMEM((n_dp, *blocks), bf16),
            dma((n_dp,)),
            dma((n_dp,)),
            dma((n,)),
            dma((n,)),
            dma((nz,)),
            dma((nz,)),
            dma((nz,)),
            dma((nz,)),
            dma((n_dp,)),
            dma((n_dp,)),
            dma((nz,)),
            dma((nz,)),
            dma((nz,)),
            dma((nz,)),
        ],
        compiler_params=pltpu.CompilerParams(
            collective_id=1, has_side_effects=True, vmem_limit_bytes=VMEM_LIMIT
        ),
        name="combine",
    )(part, route, packed, cols, basis)

    dots = route_got[:, :EXP_DEV].reshape(experts, TOK_DEV).T
    grad_route = jnp.sum(jnp.where(chosen, dots[:, :, None], 0.0), axis=1) / route_weights
    deep, wide = rank // n_dp // LANES, ff // n_dp // LANES
    cuts = [0, deep, deep + wide, deep + 2 * wide, deep + 3 * wide, 2 * deep + 3 * wide]
    g = [grads[:, a:b] for a, b in zip(cuts, cuts[1:])]
    across = lambda t: t.transpose(0, 2, 1, 3).reshape(EXP_DEV, LANES, -1)
    along = lambda t: t.transpose(0, 1, 3, 2).reshape(EXP_DEV, -1, LANES)
    return (
        grad_input,
        grad_route,
        grad_basis,
        along(g[0]),
        across(g[1]),
        across(g[2]),
        along(g[3]),
        across(g[4]),
    )


def solution(mesh):
    split = P(("dp", "expert"), None)
    held = P("expert", None, None)
    in_specs = (split, split, P(), split, split, held, held, held, held, held)
    out_specs = (
        split,
        split,
        split,
        P("expert", "dp", None),
        P("expert", None, "dp"),
        P("expert", None, "dp"),
        P("expert", "dp", None),
        P("expert", None, "dp"),
    )
    return jax.shard_map(
        functools.partial(per_device, mesh.shape["expert"], mesh.shape["dp"]),
        mesh=mesh,
        in_specs=in_specs,
        out_specs=out_specs,
        check_vma=False,
    )
```

time: 456 us -> 142 us (0.31)
  waiting for transfers between devices: 293 us -> 0 us
  Pallas kernels: 0 us -> 127 us
  matrix products: 68.4 us -> 0 us
  local copies, waits for them, and re-layouts: 40.1 us -> 11.6 us
  starting transfers between devices: 19.1 us -> 0 us
  other arithmetic: 19.3 us -> 1.35 us
  between operations: 14.5 us -> 0.72 us
    reduce_scatter x3 -> x0, waiting for transfers between devices: 173 us -> none  [the longest x1 147 us: per_device(): lax.psum_scatter(jnp.einsum('td,tr->dr', activations, dz, preferred_eleme...]
    pallas_call x0 -> x3, Pallas kernels: none -> 127 us  [the longest x1 66.5 us: per_device(): pl.pallas_call(functools.partial(combine_kernel, n, n_dp), out_shape=(jax...]
    all_to_all x4 -> x0, waiting for transfers between devices: 96.2 us -> none  [the longest x1 35.7 us: per_device(): lax.all_to_all(send_scaled, 'expert', split_axis=0, concat_axis=0, tiled=...]
    dot_general x20 -> x0, matrix products: 68.4 us -> none  [the longest x1 10.4 us: per_device(): jnp.einsum('seck,ekf->secf', codes, up_factor, preferred_element_type=f32)]
    unnamed x9 -> x0, waiting for transfers between devices: 24.2 us -> none
    all_to_all x4 -> x0, starting transfers between devices: 18.8 us -> none  [the longest x1 6.32 us: per_device(): lax.all_to_all(send_coords, 'expert', split_axis=0, concat_axis=0, tiled=...]
    unnamed x48 -> x13, local copies, waits for them, and re-layouts: 19.5 us -> 4.28 us
    gather x2 -> x0, local copies, waits for them, and re-layouts: 10.8 us -> none  [the longest x1 5.71 us: per_device(): out_rows = got_out.reshape(experts * capacity, width)[place].astype(f32)]
  transfers between devices with their start and end apart: 10 -> 0, of which waited for: 7 -> 0; matrix products, arithmetic and copies ran while one was open for 18% -> 0% of each run, Pallas kernels for 0% -> 0%
where the time goes in v1:
time: 142 us; the launch traced here: 141 us
  Pallas kernels  127 us (89%)
  local copies, waits for them, and re-layouts  11.6 us (8%)
    pallas_call x1, Pallas kernels, per_device(): pl.pallas_call(functools.partial(combine_kernel, n, n_dp), out_shape=(jax...  66.5 us
    pallas_call x1, Pallas kernels, per_device(): pl.pallas_call(functools.partial(gather_kernel, n, n_dp), out_shape=(jax....  37.2 us
    pallas_call x1, Pallas kernels, per_device(): pl.pallas_call(functools.partial(expert_kernel, n_dp, ff // 3), grid=(n /...  23.4 us
    unnamed x13, local copies, waits for them, and re-layouts  4.28 us

profile of v1, /device:TPU:0, one launch (start us, length us, event | category | flops | bytes accessed | tf_op | source)
XLA Modules:
  0.0 140.8 jit_solution(8827808762014253475)
XLA Ops:
  0.6 0.7 select_reduce_fusion.1
  1.4 0.6 pad.4.wt
  2.0 37.2 %gather_tokens.1 = (bf16[8,2,128,512]{3,2,1,0:T(8,128)(2,1)}, f32[8,8,128]{2,1,0:T(8,128)}, bf16[4,2,128,1024]{3,2,1,0:T(8,128)(2,1)}) custom-call(bf16[128,4096]{1,0:T(8,128)(2,1)} %act.1, bf16[128,4096]{1,0:T(8,128)(2,1)} %cot.1, bf16[4096,512]{1,0:T(8,128)(2,1)} %basis.3, f32[8,8,128]{2,1,0:T(8,128)} %pad.4.wt), custom_call_target="tpu_custom_call" | custom-call | tf_op jit(solution)/shard_map/gather_tokens/pallas_call | solution.py:371
  39.2 1.8 %copy.33 = f32[8,128,8]{2,1,0:T(8,128)} copy(f32[8,128,8]{1,2,0:T(8,128)} %bitcast.27) | data formatting | bytes 65536 | tf_op jit(solution)/shard_map/transpose | solution.py:395
  41.0 23.4 %experts.1 = (bf16[8,2,128,512]{3,2,1,0:T(8,128)(2,1)}, f32[8,8,128]{2,1,0:T(8,128)}, bf16[4,2,11,128,128]{4,3,2,1,0:T(8,128)(2,1)}) custom-call(bf16[8,2,128,512]{3,2,1,0:T(8,128)(2,1)} %get-tuple-element.18.x, f32[1024,8]{1,0:T(8,128)} %bitcast.23, bf16[2,512,128]{2,1,0:T(8,128)(2,1)} %pin.1, bf16[2,128,1536]{2,1,0:T(8,128)(2,1)} %gate.1, ...), custom_call_target="tpu_custom_call" | custom-call | tf_op jit(solution)/shard_map/experts/pallas_call | solution.py:399
  64.4 0.0 copy-start.3
  64.4 0.0 copy-start.2
  64.4 66.5 %combine.1 = (bf16[128,4096]{1,0:T(8,128)(2,1)}, f32[128,512]{1,0:T(8,128)}, f32[2,11,128,128]{3,2,1,0:T(8,128)}, f32[8,8,128]{2,1,0:T(8,128)}) custom-call(bf16[8,2,128,512]{3,2,1,0:T(8,128)(2,1)} %get-tuple-element.20.part, f32[8,8,128]{2,1,0:T(8,128)} %get-tuple-element.21.route, bf16[4,2,11,128,128]{4,3,2,1,0:T(8,128)(2,1)} %get-tuple-element.22.packed, ...), custom_call_target="tpu_custom_call" | custom-call | tf_op jit(solution)/shard_map/combine/pallas_call | solution.py:427
  131.0 0.8 slice.18
  131.7 0.0 copy-done.3
  131.7 0.0 copy-done.2
  131.8 0.6 div.3
  132.4 1.6 %slice_bitcast_fusion.3 = (f32[2,128,128]{2,1,0:T(8,128)}, f32[2,128,128]{1,2,0:T(8,128)S(1)}) fusion(f32[2,11,128,128]{3,2,1,0:T(8,128)} %get-tuple-element.27), kind=kLoop, calls=%fused_computation.3 | loop fusion | bytes 524288 | tf_op jit(solution)/shard_map/reshape;transpose | solution.py:472
  134.0 1.3 slice_bitcast_fusion
  135.3 0.0 copy-start
  135.3 0.9 copy.36
  136.2 0.8 copy.37
  137.0 0.2 copy.35
  137.2 0.9 copy.39
  138.1 0.2 copy.34
  138.3 0.9 copy.38
  139.2 1.0 copy.42
  140.1 0.0 copy-done.1
  140.1 0.7 copy.43
  (3 shorter events, 0.0 us)
Async XLA Ops:
  64.4 67.3 %copy-start.3 = (s32[128,8]{0,1:T(8,128)S(1)}, s32[128,8]{0,1:T(8,128)}, u32[]{:S(2)}) copy-start(s32[128,8]{0,1:T(8,128)} %param.13) | copy-start | bytes 12292
  64.4 67.3 %copy-start.2 = (f32[128,8]{0,1:T(8,128)S(1)}, f32[128,8]{0,1:T(8,128)}, u32[]{:S(2)}) copy-start(f32[128,8]{0,1:T(8,128)} %param.14) | copy-start | bytes 12292
  135.3 3.9 %copy-start = (bf16[128,4096]{1,0:T(8,128)(2,1)S(1)}, bf16[128,4096]{1,0:T(8,128)(2,1)}, u32[]{:S(2)}) copy-start(bf16[128,4096]{1,0:T(8,128)(2,1)} %get-tuple-element.65) | copy-start | bytes 3145732
  137.2 3.0 %copy-start.1 = (f32[128,512]{1,0:T(8,128)S(1)}, f32[128,512]{1,0:T(8,128)}, u32[]{:S(2)}) copy-start(f32[128,512]{1,0:T(8,128)} %get-tuple-element.67) | copy-start | bytes 786436

commit v2 on v1

--- a/solution.py
+++ b/solution.py
@@ -142,6 +142,58 @@
         loop(1, n_dp, lambda d: col_copy(a, d).wait_send())
 
 
+def expert_rows(e, chunk, coords, back, we, pin, gate, up, down, pout, acc):
+    rows, rank = back.shape
+    ff = gate.shape[2]
+    scaled = (we * back).astype(bf16)
+    codes = dot(coords, pin[e]).astype(bf16)
+    d_narrow32 = dot_nt(scaled, pout[e])
+    d_narrow = d_narrow32.astype(bf16)
+    codes_t, d_narrow_t = codes.T, d_narrow.T
+    narrow32 = jnp.zeros((rows, LANES), f32)
+    d_codes32 = jnp.zeros((rows, LANES), f32)
+    for at in range(0, ff, chunk):
+        now = slice(at, at + chunk)
+        gate_pre = dot(codes, gate[e, :, now])
+        up_pre = dot(codes, up[e, :, now])
+        d_hidden = dot_nt(d_narrow, down[e, now, :])
+        sig = 0.5 * jnp.tanh(0.5 * gate_pre) + 0.5
+        active = gate_pre * sig
+        slope = sig + active * (1.0 - sig)
+        hidden = (active * up_pre).astype(bf16)
+        d_gate = (d_hidden * up_pre * slope).astype(bf16)
+        d_up = (d_hidden * active).astype(bf16)
+        narrow32 += dot(hidden, down[e, now, :])
+        d_codes32 += dot_nt(d_gate, gate[e, :, now]) + dot_nt(d_up, up[e, :, now])
+        acc[e, :, at : at + chunk] += dot(codes_t, d_gate)
+        acc[e, :, ff + at : ff + at + chunk] += dot(codes_t, d_up)
+        acc[e, :, 2 * ff + at : 2 * ff + at + chunk] += dot(d_narrow_t, hidden)
+    narrow = narrow32.astype(bf16)
+    d_codes = d_codes32.astype(bf16)
+    outcome = dot(narrow, pout[e]).astype(bf16)
+    acc[e, :, 3 * ff : 3 * ff + rank] += dot(d_codes.T, coords)
+    acc[e, :, 3 * ff + rank :] += dot(narrow.T, scaled)
+    sums = lax.dot_general(
+        jnp.ones((8, LANES), f32),
+        narrow.astype(f32) * d_narrow32,
+        (((1,), (1,)), ((), ())),
+        precision=lax.Precision.HIGHEST,
+        preferred_element_type=f32,
+    )
+    return we * outcome.astype(f32), dot_nt(d_codes, pin[e]), sums
+
+
+def pack(n_dp, ff, rank, e, acc, packed):
+    wide, deep = ff // n_dp, rank // n_dp
+    for q in range(n_dp):
+        starts = [3 * ff + q * deep + i for i in range(0, deep, LANES)]
+        for base in (0, ff, 2 * ff):
+            starts += [base + q * wide + i for i in range(0, wide, LANES)]
+        starts += [3 * ff + rank + q * deep + i for i in range(0, deep, LANES)]
+        for i, at in enumerate(starts):
+            packed[q, e, i] = acc[e, :, at : at + LANES].astype(bf16)
+
+
 def expert_kernel(n_dp, chunk, x, w, pin, gate, up, down, pout, part, route, packed, acc):
     step = pl.program_id(0)
     nb, rank = x.shape[0], x.shape[3]
@@ -159,45 +211,11 @@
     dots = jnp.zeros((8, rows), f32)
     line = lax.broadcasted_iota(jnp.int32, (8, rows), 0)
     for e in range(EXP_DEV):
-        we = w[:, e : e + 1]
-        scaled = (we * back).astype(bf16)
-        codes = dot(coords, pin[e]).astype(bf16)
-        d_narrow32 = dot_nt(scaled, pout[e])
-        d_narrow = d_narrow32.astype(bf16)
-        codes_t, d_narrow_t = codes.T, d_narrow.T
-        narrow32 = jnp.zeros((rows, LANES), f32)
-        d_codes32 = jnp.zeros((rows, LANES), f32)
-        for at in range(0, ff, chunk):
-            now = slice(at, at + chunk)
-            gate_pre = dot(codes, gate[e, :, now])
-            up_pre = dot(codes, up[e, :, now])
-            d_hidden = dot_nt(d_narrow, down[e, now, :])
-            sig = 0.5 * jnp.tanh(0.5 * gate_pre) + 0.5
-            active = gate_pre * sig
-            slope = sig + active * (1.0 - sig)
-            hidden = (active * up_pre).astype(bf16)
-            d_gate = (d_hidden * up_pre * slope).astype(bf16)
-            d_up = (d_hidden * active).astype(bf16)
-            narrow32 += dot(hidden, down[e, now, :])
-            d_codes32 += dot_nt(d_gate, gate[e, :, now]) + dot_nt(d_up, up[e, :, now])
-            acc[e, :, at : at + chunk] += dot(codes_t, d_gate)
-            acc[e, :, ff + at : ff + at + chunk] += dot(codes_t, d_up)
-            acc[e, :, 2 * ff + at : 2 * ff + at + chunk] += dot(d_narrow_t, hidden)
-        narrow = narrow32.astype(bf16)
-        d_codes = d_codes32.astype(bf16)
-        outcome = dot(narrow, pout[e]).astype(bf16)
-        mixed += we * outcome.astype(f32)
-        dz += dot_nt(d_codes, pin[e])
-        acc[e, :, 3 * ff : 3 * ff + rank] += dot(d_codes.T, coords)
-        acc[e, :, 3 * ff + rank :] += dot(narrow.T, scaled)
-        product = narrow.astype(f32) * d_narrow32
-        sums = lax.dot_general(
-            jnp.ones((8, LANES), f32),
-            product,
-            (((1,), (1,)), ((), ())),
-            precision=lax.Precision.HIGHEST,
-            preferred_element_type=f32,
+        m, g, sums = expert_rows(
+            e, chunk, coords, back, w[:, e : e + 1], pin, gate, up, down, pout, acc
         )
+        mixed += m
+        dz += g
         dots = jnp.where(line == e, sums, dots)
     part[:, 0] = dz.astype(bf16).reshape(nb, TOK_DEV, rank)
     part[:, 1] = mixed.astype(bf16).reshape(nb, TOK_DEV, rank)
@@ -206,15 +224,8 @@
 
     @pl.when(step == pl.num_programs(0) - 1)
     def _():
-        wide, deep = ff // n_dp, rank // n_dp
-        for q in range(n_dp):
-            for e in range(EXP_DEV):
-                starts = [3 * ff + q * deep + i for i in range(0, deep, LANES)]
-                for base in (0, ff, 2 * ff):
-                    starts += [base + q * wide + i for i in range(0, wide, LANES)]
-                starts += [3 * ff + rank + q * deep + i for i in range(0, deep, LANES)]
-                for i, at in enumerate(starts):
-                    packed[q, e, i] = acc[e, :, at : at + LANES].astype(bf16)
+        for e in range(EXP_DEV):
+            pack(n_dp, ff, rank, e, acc, packed)
 
 
 def expert_sum(n, me, part, held, landed, total, s1, r1, s2, r2):
@@ -341,33 +352,332 @@
     loop(1, n_dp, lambda d: dzm_copy(d).wait_send())
 
 
-def per_device(
-    n,
-    n_dp,
-    activations,
-    cotangent,
-    basis,
-    route_ids,
-    route_weights,
-    proj_in,
-    gate_factor,
-    up_factor,
-    down_factor,
-    proj_out,
+def crossed(z, d, nz):
+    k, bit = 0, 1
+    while bit < nz:
+        zb, db = lax.rem(z // bit, 2), lax.rem(d // bit, 2)
+        k = k + bit * (zb + db - 2 * zb * db)
+        bit *= 2
+    return k
+
+
+def layer_kernel(
+    n, n_dp, chunk,
+    act_h, cot_h, basis_h, wt, pin_h, pout_h, gate_h, up_h, down_h,
+    grad_input, grad_basis, grads, route_out,
+    act, cot, basis, pin, pout, gate, up, down,
+    x, w_in, cols, cols_t, acc, part, route, packed, grads_in,
+    held, landed, total, dzm, block, held_b, landed_b,
+    s_l, s_c, r_c, s_x, r_x, s_f, s_w, r_w, s_g, r_g, s_r, r_r,
+    s1, r1, s2, r2, s_d, r_d, t1, q1, t2, q2,
 ):
-    model, rank = basis.shape
-    ff = gate_factor.shape[2]
+    me, p = lax.axis_index("expert"), lax.axis_index("dp")
     nz = n // 2
-    experts = EXP_DEV * n
+    core, z = lax.rem(me, 2), me // 2
+    sib = me + 1 - 2 * core
+    rank = basis.shape[1]
+    ff = gate.shape[2]
+    width = act.shape[1] // n_dp
+    rows = 2 * TOK_DEV
+
+    loads = [
+        pltpu.make_async_copy(src, dst, s_l.at[i])
+        for i, (src, dst) in enumerate(
+            zip(
+                (act_h, basis_h, cot_h, pin_h, pout_h, gate_h, up_h, down_h),
+                (act, basis, cot, pin, pout, gate, up, down),
+            )
+        )
+    ]
+    for load in loads:
+        load.start()
+    greet(n, n_dp, me, p)
+
+    def w_copy(d):
+        j = lax.rem(me + d, n)
+        return remote(wt.at[j], w_in.at[me], s_w.at[d], r_w.at[me], expert=j)
+
+    loop(1, n, lambda d: w_copy(d).start())
+
+    def peer(d):
+        return crossed(z, d, nz)
+
+    def x_copy(a, d, to):
+        return remote(x.at[me, a], x.at[me, a], s_x.at[a, d], r_x.at[a, me], expert=to)
+
+    loads[0].wait()
+    loads[1].wait()
+    for a, ref in enumerate((act, cot)):
+        if a == 1:
+            loads[2].wait()
+        x[me, a] = dot(ref[...], basis[...]).astype(bf16)
+        x_copy(a, 0, sib).start()
+        loop(1, nz, lambda d: x_copy(a, d, peer(d) * 2 + core).start())
+
+    def col_copy(a, d):
+        q = lax.rem(p + d, n_dp)
+        return remote(
+            (act, cot)[a].at[:, pl.ds(pl.multiple_of(q * width, LANES), width)],
+            cols.at[p, a],
+            s_c.at[a, d],
+            r_c.at[a, p],
+            dp=q,
+        )
+
+    for a in range(2):
+        loop(1, n_dp, lambda d: col_copy(a, d).start())
+    for a, ref in enumerate((act, cot)):
+        cols[p, a] = ref[:, pl.ds(pl.multiple_of(p * width, LANES), width)]
+    w_in[me] = wt[me]
+    acc[...] = jnp.zeros_like(acc)
+
+    def w_wait(d):
+        src = lax.rem(me + n - d, n)
+        remote(wt.at[src], w_in.at[src], s_w.at[d], r_w.at[src], expert=src).wait_recv()
+
+    loop(1, n, w_wait)
+    for load in loads[3:]:
+        load.wait()
+
+    def forward(a, d):
+        src = peer(d) * 2 + core
+        return remote(x.at[src, a], x.at[src, a], s_f.at[a, d], r_x.at[a, src], expert=sib)
+
+    def from_sib(a, d):
+        src = peer(d) * 2 + 1 - core
+        return remote(x.at[src, a], x.at[src, a], s_f.at[a, d], r_x.at[a, src], expert=sib)
+
+    def to_sib(k):
+        return remote(part.at[k * 2 + 1 - core], held.at[k], s1.at[k], r1.at[k], expert=sib)
+
+    def to_line(d):
+        k = peer(d)
+        return remote(held.at[k], landed.at[z], s2.at[d], r2.at[z], expert=k * 2 + core)
+
+    def combine(d):
+        k = peer(d)
+        to_sib(k).wait_recv()
+        held[k] = (part[k * 2 + core].astype(f32) + held[k].astype(f32)).astype(bf16)
+        to_line(d).start()
+
+    def grad_copy(e, d):
+        q = lax.rem(p + d, n_dp)
+        return remote(packed.at[q, e], grads_in.at[p, e], s_g.at[e, d], r_g.at[e, p], dp=q)
+
+    def send_grads(e):
+        pack(n_dp, ff, rank, e, acc, packed)
+        loop(1, n_dp, lambda d: grad_copy(e, d).start())
+
+    line = lax.broadcasted_iota(jnp.int32, (8, rows), 0)
+    square = (TOK_DEV, TOK_DEV)
+    eye = lax.broadcasted_iota(jnp.int32, square, 0) == lax.broadcasted_iota(jnp.int32, square, 1)
+
+    def pair(d):
+        k = peer(d)
+
+        @pl.when(d > 0)
+        def _():
+            for a in range(2):
+                forward(a, d).wait_recv()
+                forward(a, d).start()
+
+        for a in range(2):
+            from_sib(a, d).wait_recv()
+        both = pl.ds(k * 2, 2)
+        coords = x[both, 0].reshape(rows, rank)
+        back = x[both, 1].reshape(rows, rank).astype(f32)
+
+        def column(e):
+            return jnp.concatenate(
+                [
+                    jnp.sum(jnp.where(eye, w_in[k * 2 + b, e : e + 1, :], 0.0), axis=1, keepdims=True)
+                    for b in range(2)
+                ],
+                axis=0,
+            )
+
+        @pl.when(d > 1)
+        def _():
+            combine(d - 1)
+
+        mixed = jnp.zeros((rows, rank), f32)
+        dz = jnp.zeros((rows, rank), f32)
+        dots = jnp.zeros((8, rows), f32)
+        for e in range(EXP_DEV):
+            m, g, sums = expert_rows(
+                e, chunk, coords, back, column(e), pin, gate, up, down, pout, acc
+            )
+            mixed += m
+            dz += g
+            dots = jnp.where(line == e, sums, dots)
+        part[both, 0] = dz.astype(bf16).reshape(2, TOK_DEV, rank)
+        part[both, 1] = mixed.astype(bf16).reshape(2, TOK_DEV, rank)
+        for b in range(2):
+            route[k * 2 + b] = dots[:, b * TOK_DEV : (b + 1) * TOK_DEV]
+        to_sib(k).start()
+
+    loop(0, nz, pair)
+    send_grads(0)
+    if nz > 1:
+        combine(nz - 1)
+
+    def route_copy(d):
+        j = lax.rem(me + d, n)
+        return remote(route.at[j], route_out.at[me], s_r.at[d], r_r.at[me], expert=j)
+
+    loop(1, n, lambda d: route_copy(d).start())
+    route_out[me] = route[me]
+    for e in range(1, EXP_DEV):
+        pack(n_dp, ff, rank, e, acc, packed)
+    to_sib(z).wait_recv()
+    total[...] = part[me].astype(f32) + held[z].astype(f32)
+
+    def collect(d):
+        k = peer(d)
+        remote(held.at[k], landed.at[k], s2.at[d], r2.at[k], expert=k * 2 + core).wait_recv()
+        total[...] += landed[k].astype(f32)
+
+    loop(1, nz, collect)
+    dzm[p] = total[...].astype(bf16)
+
+    def dzm_copy(d):
+        q = lax.rem(p + d, n_dp)
+        return remote(dzm.at[p], dzm.at[p], s_d.at[d], r_d.at[p], dp=q)
+
+    loop(1, n_dp, lambda d: dzm_copy(d).start())
+    for e in range(1, EXP_DEV):
+        loop(1, n_dp, lambda d: grad_copy(e, d).start())
+
+    def col_wait(a, d):
+        src = lax.rem(p + n_dp - d, n_dp)
+        remote(cols.at[src, a], cols.at[src, a], s_c.at[a, d], r_c.at[a, src], dp=src).wait_recv()
+
+    for a in range(2):
+        loop(1, n_dp, lambda d: col_wait(a, d))
+    for q in range(n_dp):
+        for a in range(2):
+            at = (q * 2 + a) * TOK_DEV
+            cols_t[:, at : at + TOK_DEV] = cols[q, a].T
+    grad_input[...] = dot_nt(dzm[p, 0], basis[...]).astype(bf16)
+
+    def dzm_wait(d):
+        src = lax.rem(p + n_dp - d, n_dp)
+        remote(dzm.at[src], dzm.at[src], s_d.at[d], r_d.at[src], dp=src).wait_recv()
+
+    loop(1, n_dp, dzm_wait)
+    sums = dot(cols_t[...], dzm[...].reshape(n_dp * rows, rank))
+    block[...] = sums.astype(bf16).reshape(block.shape)
+    expert_sum(n, me, block, held_b, landed_b, grad_basis, t1, q1, t2, q2)
+
+    def grad_wait(e, d):
+        src = lax.rem(p + n_dp - d, n_dp)
+        remote(
+            grads_in.at[src, e], grads_in.at[src, e], s_g.at[e, d], r_g.at[e, src], dp=src
+        ).wait_recv()
+        grads[e] += grads_in[src, e].astype(f32)
+
+    for e in range(EXP_DEV):
+        grads[e] = packed[p, e].astype(f32)
+        loop(1, n_dp, lambda d: grad_wait(e, d))
+
+    def route_wait(d):
+        src = lax.rem(me + n - d, n)
+        remote(route.at[src], route_out.at[src], s_r.at[d], r_r.at[src], expert=src).wait_recv()
+
+    loop(1, n, route_wait)
+    loop(1, n, lambda d: route_copy(d).wait_send())
+    loop(1, n, lambda d: w_copy(d).wait_send())
+    for a in range(2):
+        x_copy(a, 0, sib).wait_send()
+        loop(1, nz, lambda d: x_copy(a, d, peer(d) * 2 + core).wait_send())
+        loop(1, nz, lambda d: forward(a, d).wait_send())
+        loop(1, n_dp, lambda d: col_copy(a, d).wait_send())
+    loop(0, nz, lambda k: to_sib(k).wait_send())
+    loop(1, nz, lambda d: to_line(d).wait_send())
+    loop(1, n_dp, lambda d: dzm_copy(d).wait_send())
+    for e in range(EXP_DEV):
+        loop(1, n_dp, lambda d: grad_copy(e, d).wait_send())
+
+
+def finish_kernel(
+    gi, gb, grads, grad_input, grad_basis, g_in, g_gate, g_up, g_down, g_out,
+):
+    grad_input[...] = gi[...]
+    grad_basis[...] = gb[...]
+    deep, wide = g_in.shape[1] // LANES, g_gate.shape[2] // LANES
+    for e in range(EXP_DEV):
+        for i in range(deep):
+            at = slice(i * LANES, (i + 1) * LANES)
+            g_in[e, at, :] = grads[e, i].T
+            g_out[e, :, at] = grads[e, deep + 3 * wide + i]
+        for i in range(wide):
+            at = slice(i * LANES, (i + 1) * LANES)
+            g_gate[e, :, at] = grads[e, deep + i]
+            g_up[e, :, at] = grads[e, deep + wide + i]
+            g_down[e, at, :] = grads[e, deep + 2 * wide + i].T
+
+
+def whole_layer(n, n_dp, shapes, blocks, arrays, wt):
+    model, rank, ff = shapes
+    nz = n // 2
+    width = model // n_dp
+    rows_b = width // n
+    vmem = pl.BlockSpec(memory_space=pltpu.VMEM)
+    hbm = pl.BlockSpec(memory_space=pl.ANY)
+    dma = pltpu.SemaphoreType.DMA
+    act, cot, basis, *weights = arrays
+    token = (TOK_DEV, rank)
+    return pl.pallas_call(
+        functools.partial(layer_kernel, n, n_dp, ff // 3),
+        out_shape=(
+            jax.ShapeDtypeStruct((TOK_DEV, model), bf16),
+            jax.ShapeDtypeStruct((rows_b, rank), f32),
+            jax.ShapeDtypeStruct(blocks, f32),
+            jax.ShapeDtypeStruct((n, 8, TOK_DEV), f32),
+        ),
+        in_specs=[hbm] * 3 + [vmem] + [hbm] * 5,
+        out_specs=(vmem,) * 4,
+        scratch_shapes=[pltpu.VMEM(a.shape, bf16) for a in arrays]
+        + [
+            pltpu.VMEM((n, 2, *token), bf16),
+            pltpu.VMEM((n, 8, TOK_DEV), f32),
+            pltpu.VMEM((n_dp, 2, TOK_DEV, width), bf16),
+            pltpu.VMEM((width, n_dp * 2 * TOK_DEV), bf16),
+            pltpu.VMEM((EXP_DEV, LANES, 3 * ff + 2 * rank), f32),
+            pltpu.VMEM((n, 2, *token), bf16),
+            pltpu.VMEM((n, 8, TOK_DEV), f32),
+            pltpu.VMEM((n_dp, *blocks), bf16),
+            pltpu.VMEM((n_dp, *blocks), bf16),
+            pltpu.VMEM((nz, 2, *token), bf16),
+            pltpu.VMEM((nz, 2, *token), bf16),
+            pltpu.VMEM((2, *token), f32),
+            pltpu.VMEM((n_dp, 2, *token), bf16),
+            pltpu.VMEM((n, rows_b, rank), bf16),
+            pltpu.VMEM((nz, rows_b, rank), bf16),
+            pltpu.VMEM((nz, rows_b, rank), bf16),
+        ]
+        + [
+            dma(s)
+            for s in (
+                (8,), (2, n_dp), (2, n_dp), (2, nz), (2, n), (2, nz), (n,), (n,),
+                (EXP_DEV, n_dp), (EXP_DEV, n_dp), (n,), (n,),
+                (nz,), (nz,), (nz,), (nz,), (n_dp,), (n_dp,), (nz,), (nz,), (nz,), (nz,),
+            )
+        ],
+        compiler_params=pltpu.CompilerParams(
+            collective_id=2, has_side_effects=True, vmem_limit_bytes=VMEM_LIMIT
+        ),
+        name="whole_layer",
+    )(act, cot, basis, wt, *weights)
+
+
+def staged_layer(n, n_dp, shapes, blocks, arrays, wt):
+    model, rank, ff = shapes
+    nz = n // 2
     width = model // n_dp
     vmem = pl.BlockSpec(memory_space=pltpu.VMEM)
     dma = pltpu.SemaphoreType.DMA
-
-    chosen = route_ids[:, None, :] == jnp.arange(experts, dtype=jnp.int32)[None, :, None]
-    dense = jnp.sum(jnp.where(chosen, route_weights[:, None, :], 0.0), axis=2)
-    wt = dense.T.reshape(n, EXP_DEV, TOK_DEV)
-    wt = jnp.pad(wt, ((0, 0), (0, 8 - EXP_DEV), (0, 0)))
-
+    activations, cotangent, basis, proj_in, proj_out, gate_factor, up_factor, down_factor = arrays
     x, w_all, cols = pl.pallas_call(
         functools.partial(gather_kernel, n, n_dp),
         out_shape=(
@@ -394,7 +704,6 @@
 
     w_rows = w_all.transpose(0, 2, 1).reshape(n * TOK_DEV, 8)
     nb = 2
-    blocks = EXP_DEV, (2 * rank + 3 * ff) // n_dp // LANES, LANES, LANES
     whole = lambda a: pl.BlockSpec(a.shape, lambda i: (0,) * a.ndim)
     part, route, packed = pl.pallas_call(
         functools.partial(expert_kernel, n_dp, ff // 3),
@@ -424,7 +733,7 @@
     )(x, w_rows, proj_in, gate_factor, up_factor, down_factor, proj_out)
 
     rows_b = width // n
-    grad_input, grad_basis, grads, route_got = pl.pallas_call(
+    return pl.pallas_call(
         functools.partial(combine_kernel, n, n_dp),
         out_shape=(
             jax.ShapeDtypeStruct((TOK_DEV, model), bf16),
@@ -464,23 +773,57 @@
         name="combine",
     )(part, route, packed, cols, basis)
 
-    dots = route_got[:, :EXP_DEV].reshape(experts, TOK_DEV).T
+
+def per_device(
+    n,
+    n_dp,
+    activations,
+    cotangent,
+    basis,
+    route_ids,
+    route_weights,
+    proj_in,
+    gate_factor,
+    up_factor,
+    down_factor,
+    proj_out,
+):
+    model, rank = basis.shape
+    ff = gate_factor.shape[2]
+    experts = EXP_DEV * n
+
+    chosen = route_ids[:, None, :] == jnp.arange(experts, dtype=jnp.int32)[None, :, None]
+    dense = jnp.sum(jnp.where(chosen, route_weights[:, None, :], 0.0), axis=2)
+    wt = dense.T.reshape(n, EXP_DEV, TOK_DEV)
+    wt = jnp.pad(wt, ((0, 0), (0, 8 - EXP_DEV), (0, 0)))
+
+    blocks = EXP_DEV, (2 * rank + 3 * ff) // n_dp // LANES, LANES, LANES
+    arrays = activations, cotangent, basis, proj_in, proj_out, gate_factor, up_factor, down_factor
+    tokens = n * TOK_DEV * rank * 2
+    fits = 6 * tokens + 34 * 1024 * 1024 < VMEM_LIMIT and (n & (n - 1)) == 0
+    layer = whole_layer if fits else staged_layer
+    grad_input, grad_basis, grads, dots = layer(n, n_dp, (model, rank, ff), blocks, arrays, wt)
+    deep, wide = rank // n_dp, ff // n_dp
+    vmem = pl.BlockSpec(memory_space=pltpu.VMEM)
+    grad_input, grad_basis, *factors = pl.pallas_call(
+        finish_kernel,
+        out_shape=(
+            jax.ShapeDtypeStruct(grad_input.shape, bf16),
+            jax.ShapeDtypeStruct(grad_basis.shape, f32),
+            jax.ShapeDtypeStruct((EXP_DEV, deep, LANES), f32),
+            jax.ShapeDtypeStruct((EXP_DEV, LANES, wide), f32),
+            jax.ShapeDtypeStruct((EXP_DEV, LANES, wide), f32),
+            jax.ShapeDtypeStruct((EXP_DEV, wide, LANES), f32),
+            jax.ShapeDtypeStruct((EXP_DEV, LANES, deep), f32),
+        ),
+        in_specs=[vmem] * 3,
+        out_specs=(vmem,) * 7,
+        compiler_params=pltpu.CompilerParams(vmem_limit_bytes=VMEM_LIMIT),
+        name="finish",
+    )(grad_input, grad_basis, grads)
+    dots = dots[:, :EXP_DEV].reshape(experts, TOK_DEV).T
     grad_route = jnp.sum(jnp.where(chosen, dots[:, :, None], 0.0), axis=1) / route_weights
-    deep, wide = rank // n_dp // LANES, ff // n_dp // LANES
-    cuts = [0, deep, deep + wide, deep + 2 * wide, deep + 3 * wide, 2 * deep + 3 * wide]
-    g = [grads[:, a:b] for a, b in zip(cuts, cuts[1:])]
-    across = lambda t: t.transpose(0, 2, 1, 3).reshape(EXP_DEV, LANES, -1)
-    along = lambda t: t.transpose(0, 1, 3, 2).reshape(EXP_DEV, -1, LANES)
-    return (
-        grad_input,
-        grad_route,
-        grad_basis,
-        along(g[0]),
-        across(g[1]),
-        across(g[2]),
-        along(g[3]),
-        across(g[4]),
-    )
+    return (grad_input, grad_route, grad_basis, *factors)
 
 
 def solution(mesh):

time: 142 us -> 97.8 us (0.69)
  Pallas kernels: 127 us -> 93.2 us
  local copies, waits for them, and re-layouts: 11.6 us -> 1.39 us
    pallas_call x3 -> x2, Pallas kernels: 127 us -> 93.2 us  [the longest x1 89.8 us: whole_layer(): pl.pallas_call(functools.partial(layer_kernel, n, n_dp, ff // 3), out_sha...]
    transpose x5 -> x0, local copies, waits for them, and re-layouts: 4.3 us -> none  [the longest x2 2.22 us: per_device(): along = lambda t: t.transpose(0, 1, 3, 2).reshape(EXP_DEV, -1, LANES)]
    unnamed x13 -> x4, local copies, waits for them, and re-layouts: 4.28 us -> 0.01 us
    another operation x1 -> x0, local copies, waits for them, and re-layouts: 1.64 us -> none  [per_device(): across = lambda t: t.transpose(0, 2, 1, 3).reshape(EXP_DEV, LANES, -1)]
where the time goes in v2:
time: 97.8 us; the launch traced here: 96.6 us
  Pallas kernels  93.2 us (95%)
  local copies, waits for them, and re-layouts  1.39 us (1%)
  other arithmetic  1.35 us (1%)
    pallas_call x1, Pallas kernels, whole_layer(): pl.pallas_call(functools.partial(layer_kernel, n, n_dp, ff // 3), out_sha...  89.8 us
    pallas_call x1, Pallas kernels, per_device(): pl.pallas_call(finish_kernel, out_shape=(jax.ShapeDtypeStruct(grad_input....  3.43 us

profile of v2, /device:TPU:0, one launch (start us, length us, event | category | flops | bytes accessed | tf_op | source)
XLA Modules:
  0.0 96.6 jit_solution(11960859416392974763)
XLA Ops:
  0.6 0.7 select_reduce_fusion.1
  1.4 0.6 pad.4.wt
  2.0 0.0 copy-start.1
  2.0 0.0 copy-start
  2.0 89.8 %whole_layer.1 = (bf16[128,4096]{1,0:T(8,128)(2,1)}, f32[128,512]{1,0:T(8,128)}, f32[2,11,128,128]{3,2,1,0:T(8,128)}, f32[8,8,128]{2,1,0:T(8,128)}) custom-call(bf16[128,4096]{1,0:T(8,128)(2,1)} %act_h.1, bf16[128,4096]{1,0:T(8,128)(2,1)} %cot_h.1, bf16[4096,512]{1,0:T(8,128)(2,1)} %basis_h.1, f32[8,8,128]{2,1,0:T(8,128)} %pad.4.wt, ...), custom_call_target="tpu_custom_call" | custom-call | tf_op jit(solution)/shard_map/whole_layer/pallas_call | solution.py:630
  91.8 3.4 %finish.1 = (bf16[128,4096]{1,0:T(8,128)(2,1)}, f32[128,512]{1,0:T(8,128)}, f32[2,128,128]{2,1,0:T(8,128)}, f32[2,128,384]{2,1,0:T(8,128)}, f32[2,128,384]{2,1,0...) custom-call(bf16[128,4096]{1,0:T(8,128)(2,1)} %get-tuple-element.19.gi, f32[128,512]{1,0:T(8,128)} %get-tuple-element.20.gb, ...), custom_call_target="tpu_custom_call" | custom-call | tf_op jit(solution)/shard_map/finish/pallas_call | solution.py:808
  95.2 0.8 slice.3
  96.0 0.0 copy-done.1
  96.0 0.0 copy-done
  96.0 0.6 div.3
  (1 shorter events, 0.0 us)
Async XLA Ops:
  2.0 94.0 %copy-start.1 = (s32[128,8]{0,1:T(8,128)S(1)}, s32[128,8]{0,1:T(8,128)}, u32[]{:S(2)}) copy-start(s32[128,8]{0,1:T(8,128)} %param.13) | copy-start | bytes 12292
  2.0 94.0 %copy-start = (f32[128,8]{0,1:T(8,128)S(1)}, f32[128,8]{0,1:T(8,128)}, u32[]{:S(2)}) copy-start(f32[128,8]{0,1:T(8,128)} %param.14) | copy-start | bytes 12292

commit v3 on v2

--- a/solution.py
+++ b/solution.py
@@ -405,6 +405,14 @@
     def x_copy(a, d, to):
         return remote(x.at[me, a], x.at[me, a], s_x.at[a, d], r_x.at[a, me], expert=to)
 
+    near = 3 if nz == 4 else nz
+
+    def relay(a):
+        src = peer(2) * 2 + core
+        return remote(
+            x.at[src, a], x.at[src, a], s_x.at[a, 3], r_x.at[a, src], expert=peer(1) * 2 + core
+        )
+
     loads[0].wait()
     loads[1].wait()
     for a, ref in enumerate((act, cot)):
@@ -412,7 +420,7 @@
             loads[2].wait()
         x[me, a] = dot(ref[...], basis[...]).astype(bf16)
         x_copy(a, 0, sib).start()
-        loop(1, nz, lambda d: x_copy(a, d, peer(d) * 2 + core).start())
+        loop(1, near, lambda d: x_copy(a, d, peer(d) * 2 + core).start())
 
     def col_copy(a, d):
         q = lax.rem(p + d, n_dp)
@@ -464,9 +472,11 @@
         q = lax.rem(p + d, n_dp)
         return remote(packed.at[q, e], grads_in.at[p, e], s_g.at[e, d], r_g.at[e, p], dp=q)
 
+    early = max(1, n_dp - 1)
+
     def send_grads(e):
         pack(n_dp, ff, rank, e, acc, packed)
-        loop(1, n_dp, lambda d: grad_copy(e, d).start())
+        loop(1, early, lambda d: grad_copy(e, d).start())
 
     line = lax.broadcasted_iota(jnp.int32, (8, rows), 0)
     square = (TOK_DEV, TOK_DEV)
@@ -480,6 +490,13 @@
             for a in range(2):
                 forward(a, d).wait_recv()
                 forward(a, d).start()
+
+        if near < nz:
+
+            @pl.when(d == 2)
+            def _():
+                for a in range(2):
+                    relay(a).start()
 
         for a in range(2):
             from_sib(a, d).wait_recv()
@@ -545,6 +562,7 @@
         return remote(dzm.at[p], dzm.at[p], s_d.at[d], r_d.at[p], dp=q)
 
     loop(1, n_dp, lambda d: dzm_copy(d).start())
+    loop(early, n_dp, lambda d: grad_copy(0, d).start())
     for e in range(1, EXP_DEV):
         loop(1, n_dp, lambda d: grad_copy(e, d).start())
 
@@ -589,7 +607,9 @@
     loop(1, n, lambda d: w_copy(d).wait_send())
     for a in range(2):
         x_copy(a, 0, sib).wait_send()
-        loop(1, nz, lambda d: x_copy(a, d, peer(d) * 2 + core).wait_send())
+        loop(1, near, lambda d: x_copy(a, d, peer(d) * 2 + core).wait_send())
+        if near < nz:
+            relay(a).wait_send()
         loop(1, nz, lambda d: forward(a, d).wait_send())
         loop(1, n_dp, lambda d: col_copy(a, d).wait_send())
     loop(0, nz, lambda k: to_sib(k).wait_send())

time: 97.8 us -> 105 us (1.074)
  the two profiles are of different devices: /device:TPU:0 before, /device:TPU:10 now
where the time goes in v3:
time: 105 us
  Pallas kernels  101 us (96%)
  local copies, waits for them, and re-layouts  1.39 us (1%)
  other arithmetic  1.35 us (1%)
    pallas_call x1, Pallas kernels, whole_layer(): pl.pallas_call(functools.partial(layer_kernel, n, n_dp, ff // 3), out_sha...  97.7 us
    pallas_call x1, Pallas kernels, per_device(): pl.pallas_call(finish_kernel, out_shape=(jax.ShapeDtypeStruct(grad_input....  3.43 us

profile of v3, /device:TPU:10, one launch (start us, length us, event | category | flops | bytes accessed | tf_op | source)
XLA Modules:
  0.0 104.5 jit_solution(15767860809387404087)
XLA Ops:
  0.6 0.7 select_reduce_fusion.1
  1.4 0.6 pad.4.wt
  2.0 0.0 copy-start.1
  2.0 0.0 copy-start
  2.0 97.7 %whole_layer.1 = (bf16[128,4096]{1,0:T(8,128)(2,1)}, f32[128,512]{1,0:T(8,128)}, f32[2,11,128,128]{3,2,1,0:T(8,128)}, f32[8,8,128]{2,1,0:T(8,128)}) custom-call(bf16[128,4096]{1,0:T(8,128)(2,1)} %act_h.1, bf16[128,4096]{1,0:T(8,128)(2,1)} %cot_h.1, bf16[4096,512]{1,0:T(8,128)(2,1)} %basis_h.1, f32[8,8,128]{2,1,0:T(8,128)} %pad.4.wt, ...), custom_call_target="tpu_custom_call" | custom-call | tf_op jit(solution)/shard_map/whole_layer/pallas_call | solution.py:650
  99.7 3.4 %finish.1 = (bf16[128,4096]{1,0:T(8,128)(2,1)}, f32[128,512]{1,0:T(8,128)}, f32[2,128,128]{2,1,0:T(8,128)}, f32[2,128,384]{2,1,0:T(8,128)}, f32[2,128,384]{2,1,0...) custom-call(bf16[128,4096]{1,0:T(8,128)(2,1)} %get-tuple-element.19.gi, f32[128,512]{1,0:T(8,128)} %get-tuple-element.20.gb, ...), custom_call_target="tpu_custom_call" | custom-call | tf_op jit(solution)/shard_map/finish/pallas_call | solution.py:828
  103.2 0.8 slice.3
  103.9 0.0 copy-done.1
  103.9 0.0 copy-done
  103.9 0.6 div.3
  (1 shorter events, 0.0 us)
Async XLA Ops:
  2.0 101.9 %copy-start.1 = (s32[128,8]{0,1:T(8,128)S(1)}, s32[128,8]{0,1:T(8,128)}, u32[]{:S(2)}) copy-start(s32[128,8]{0,1:T(8,128)} %param.13) | copy-start | bytes 12292
  2.0 102.0 %copy-start = (f32[128,8]{0,1:T(8,128)S(1)}, f32[128,8]{0,1:T(8,128)}, u32[]{:S(2)}) copy-start(f32[128,8]{0,1:T(8,128)} %param.14) | copy-start | bytes 12292
